TPU v7x, 32 devices: a whole 2x2x4 slice. The times are simulated.
32 devices in a mesh: group: 2 (over core), dp: 4 (over y, x), tensor: 4 (over z).
Axes of the slice: x: 2, y: 2, z: 4, core: 2. Of those that a mesh axis runs over, the one named last changes fastest.
Arguments:
- stream: bfloat16 [32, 8192], P('tensor', ('group', 'dp'))
- norm_attn: bfloat16 [8192], P(('group', 'dp')), may hold values from 0.29882812 to 3
- norm_ffn: bfloat16 [8192], P(('group', 'dp')), may hold values from 0.29882812 to 3
- w_query: bfloat16 [8192, 8192], P(('group', 'dp'), 'tensor'), may hold values from -0.0625 to 0.0625
- w_keyval: bfloat16 [8192, 2048], P(('group', 'dp'), 'tensor'), may hold values from -0.0625 to 0.0625
- w_out: bfloat16 [8192, 8192], P('tensor', ('group', 'dp')), may hold values from -0.0625 to 0.0625
- w_gate: bfloat16 [8192, 28672], P(('group', 'dp'), 'tensor'), may hold values from -0.0625 to 0.0625
- w_up: bfloat16 [8192, 28672], P(('group', 'dp'), 'tensor'), may hold values from -0.0625 to 0.0625
- w_down: bfloat16 [28672, 8192], P('tensor', ('group', 'dp')), may hold values from -0.03125 to 0.03125
- cache: bfloat16 [32, 8, 256, 256], P(('group', 'dp'), 'tensor')
- lengths: int32 [32], P(('group', 'dp')), may hold values from 1 to 256, as said below
- location: int32 [32], P(('group', 'dp')), may hold values from 0 to 31, as said below
Outputs:
- updated: float32 [32, 8192], P('tensor', ('group', 'dp'))
Inputs may be any that keep to these rules, and one draw needn't show every extreme that they name: Each of the 32 slots is named by exactly one request. Slot s belongs to owner s // 4. Requests r of one aligned block of 4 (one device's requests) that share an owner have different values of location modulo 2; in every draw 2 of them share an owner. `lengths`: some slot holds 256 valid positions in every draw.
All inputs are finite; a program needn't handle non-finite values.
Results may differ from a plain program's by a relative error of at most 0.005.
The roundings to bfloat16 on the way count: a program that leaves them out, or rounds other values in their place, can miss the bound.
Values may be sent and summed in bfloat16 or wider, within the bound.
A program may use at most 128 MiB of HBM per device.

v0:
```python
import jax
import jax.numpy as jnp
from jax import lax
from jax.sharding import PartitionSpec as P

D = 8192
CAP = 2


EPSILON = 1e-05


def normed(values, gain):
    squares = lax.psum(jnp.sum(values * values, axis=1), ("group", "dp"))
    scale = lax.rsqrt(squares / D + EPSILON)
    return (values * scale[:, None] * gain.astype(jnp.float32)[None, :]).astype(jnp.bfloat16)


def width_sum(normal_rows, matrices):
    gathered = lax.all_gather(normal_rows, "tensor", axis=0, tiled=True)
    return lax.psum_scatter(
        jnp.concatenate(
            [jnp.dot(gathered, matrix, preferred_element_type=jnp.float32) for matrix in matrices],
            axis=1,
        ),
        ("group", "dp"),
        scatter_dimension=0,
        tiled=True,
    )


def project_rows(local_rows, matrix):
    partial_sum = jnp.dot(
        lax.all_gather(local_rows, ("group", "dp"), axis=0, tiled=True),
        matrix,
        preferred_element_type=jnp.float32,
    )
    return lax.psum_scatter(partial_sum, "tensor", scatter_dimension=0, tiled=True)


def attend(query, fresh, stored, counts):
    items = query.shape[0]
    kv_local = stored.shape[1]
    head_size = stored.shape[3] // 2
    grouped = query.reshape(items, kv_local, -1, head_size)
    fresh = fresh.reshape(items, kv_local, 2 * head_size)
    scale = head_size ** (-0.5)
    scores = (
        jnp.einsum(
            "mkgd,mkpd->mkgp", grouped, stored[..., :head_size], preferred_element_type=jnp.float32
        )
        * scale
    )
    own = (
        jnp.einsum(
            "mkgd,mkd->mkg", grouped, fresh[..., :head_size], preferred_element_type=jnp.float32
        )
        * scale
    )
    place = jnp.arange(stored.shape[2], dtype=jnp.int32)
    valid = place[None, None, None, :] < counts[:, None, None, None]
    top = jnp.maximum(jnp.max(jnp.where(valid, scores, -1e30), axis=3), own)
    expo = jnp.where(valid, jnp.exp(scores - top[..., None]), 0.0)
    own_expo = jnp.exp(own - top)
    total = jnp.sum(expo, axis=3) + own_expo
    probs = (expo / total[..., None]).astype(jnp.bfloat16)
    own_prob = (own_expo / total).astype(jnp.bfloat16)
    mixed = jnp.einsum(
        "mkgp,mkpd->mkgd", probs, stored[..., head_size:], preferred_element_type=jnp.float32
    )
    mixed = mixed + own_prob.astype(jnp.float32)[..., None] * fresh[:, :, None, head_size:].astype(
        jnp.float32
    )
    return mixed.reshape(items, -1).astype(jnp.bfloat16)


def per_device(
    stream,
    norm_attn,
    norm_ffn,
    w_query,
    w_keyval,
    w_out,
    w_gate,
    w_up,
    w_down,
    cache,
    lengths,
    location,
):
    owners = lax.axis_size(("group", "dp"))
    per_owner = cache.shape[0]
    resid = stream.astype(jnp.float32)
    attn_in = normed(resid, norm_attn)
    joined = width_sum(attn_in, (w_query, w_keyval))
    query_cols = w_query.shape[1]
    query = joined[:, :query_cols].astype(jnp.bfloat16)
    fresh = joined[:, query_cols:].astype(jnp.bfloat16)
    fresh_cols = fresh.shape[1]
    target = location // per_owner
    place = target * CAP + location % per_owner % CAP
    slot = location % per_owner
    send_query = (
        jnp.zeros((owners * CAP, query_cols), jnp.bfloat16)
        .at[place]
        .set(query)
        .reshape(owners, CAP, query_cols)
    )
    send_fresh = (
        jnp.zeros((owners * CAP, fresh_cols), jnp.bfloat16)
        .at[place]
        .set(fresh)
        .reshape(owners, CAP, fresh_cols)
    )
    send_slot = jnp.zeros((owners * CAP,), jnp.int32).at[place].set(slot).reshape(owners, CAP)
    got_query = lax.all_to_all(send_query, ("group", "dp"), split_axis=0, concat_axis=0, tiled=True)
    got_fresh = lax.all_to_all(send_fresh, ("group", "dp"), split_axis=0, concat_axis=0, tiled=True)
    got_slot = lax.all_to_all(send_slot, ("group", "dp"), split_axis=0, concat_axis=0, tiled=True)
    sources = got_slot.shape[0]
    count = got_slot.shape[1]
    flat_slot = got_slot.reshape(-1)
    answer = attend(
        got_query.reshape(sources * count, -1),
        got_fresh.reshape(sources * count, -1),
        cache[flat_slot],
        lengths[flat_slot],
    )
    answer = answer.reshape(sources, count, -1)
    returned = lax.all_to_all(answer, ("group", "dp"), split_axis=0, concat_axis=0, tiled=True)
    attended = returned.reshape(owners * CAP, -1)[place]
    middle = resid + project_rows(attended, w_out)
    ffn_in = normed(middle, norm_ffn)
    both = width_sum(ffn_in, (w_gate, w_up))
    hidden_cols = w_gate.shape[1]
    hidden = (jax.nn.silu(both[:, :hidden_cols]) * both[:, hidden_cols:]).astype(jnp.bfloat16)
    return middle + project_rows(hidden, w_down)


def solution(mesh):
    placed = (
        P("tensor", ("group", "dp")),
        P(("group", "dp")),
        P(("group", "dp")),
        P(("group", "dp"), "tensor"),
        P(("group", "dp"), "tensor"),
        P("tensor", ("group", "dp")),
        P(("group", "dp"), "tensor"),
        P(("group", "dp"), "tensor"),
        P("tensor", ("group", "dp")),
        P(("group", "dp"), "tensor", None, None),
        P(("group", "dp")),
        P(("group", "dp")),
    )
    return jax.shard_map(
        per_device,
        mesh=mesh,
        in_specs=placed,
        out_specs=P("tensor", ("group", "dp")),
        check_vma=False,
    )
```

profile of v0, /device:TPU:0, one launch (start us, length us, event | category | flops | bytes accessed | tf_op | source)
XLA Modules:
  0.0 327.9 jit_solution(11928510455228937460)
XLA Ops:
  8.6 5.2 %all-to-all-start = ((s32[8,1,2]{2,1,0:T(1,128)}), s32[8,1,2]{2,1,0:T(1,128)S(1)}, u32[]{:S(2)}, u32[]{:S(2)}) async-start(s32[8,1,2]{2,1,0:T(1,128)} %bitcast), calls=%async_computation | async-start | bytes 8192 | tf_op jit(solution)/shard_map/all_to_all | solution.py:118
  15.3 14.8 %psum.14 = f32[8]{0:T(128)S(1)} all-reduce(f32[8]{0:T(128)S(1)} %fusion.21), channel_id=1, replica_groups=mesh['group'=2,'dp'=4,'tensor'=4] {'group','dp'}, use_global_device_ids=true, to_apply=%region_2.0 | all-reduce | flops 8 | bytes 64 | tf_op jit(solution)/shard_map/psum | solution.py:14
  30.9 13.4 %all_gather.12 = bf16[32,1024]{1,0:T(8,128)(2,1)S(1)} all-gather(bf16[8,1024]{1,0:T(8,128)(2,1)S(1)} %fusion.23), channel_id=1, replica_groups=mesh['group'=2,'dp'=4,'tensor'=4] {'tensor'}, dimensions={0}, use_global_device_ids=true | all-gather | bytes 81920 | tf_op jit(solution)/shard_map/all_gather | solution.py:20
  44.3 3.0 fusion.41
  47.6 33.5 %all-reduce.6 = bf16[32,2560]{1,0:T(8,128)(2,1)S(1)} all-reduce(f32[32,2560]{1,0:T(8,128)S(1)} %pad_maximum_fusion.1), channel_id=3, replica_groups=mesh['group'=2,'dp'=4,'tensor'=4] {'group','dp'}, use_global_device_ids=true, to_apply=%region_3.4.clone | all-reduce | flops 81920 | bytes 491520
  85.0 3.3 %all-to-all-start.2 = ((bf16[8,2,512]{2,1,0:T(2,128)(2,1)}), bf16[8,2,512]{2,1,0:T(2,128)(2,1)S(1)}, u32[]{:S(2)}, u32[]{:S(2)}) async-start(bf16[8,2,512]{2,1,0:T(2,128)(2,1)} %reshape.81), calls=%async_computation.2 | async-start | bytes 32768 | tf_op jit(solution)/shard_map/all_to_all | solution.py:117
  90.4 2.7 gather_fusion.1
  93.2 4.1 %all-to-all-start.1 = ((bf16[8,2,2048]{2,1,0:T(2,128)(2,1)}), bf16[8,2,2048]{2,1,0:T(2,128)(2,1)S(1)}, u32[]{:S(2)}, u32[]{:S(2)}) async-start(bf16[8,2,2048]{2,1,0:T(2,128)(2,1)} %reshape.80), calls=%async_computation.1 | async-start | bytes 131072 | tf_op jit(solution)/shard_map/all_to_all | solution.py:116
  97.4 4.9 %all-to-all-done.1 = bf16[8,2,2048]{2,1,0:T(2,128)(2,1)S(1)} async-done(((bf16[8,2,2048]{2,1,0:T(2,128)(2,1)}), bf16[8,2,2048]{2,1,0:T(2,128)(2,1)S(1)}, u32[]{:S(2)}, u32[]{:S(2)}) %all-to-all-start.1) | async-done | bytes 65568 | tf_op jit(solution)/shard_map/all_to_all | solution.py:116
  102.4 2.3 select_reduce_fusion
  105.1 2.0 fusion.10
  107.8 3.3 %all-to-all-start.3 = ((bf16[8,2,2048]{2,1,0:T(2,128)(2,1)}), bf16[8,2,2048]{2,1,0:T(2,128)(2,1)S(1)}, u32[]{:S(2)}, u32[]{:S(2)}) async-start(bf16[8,2,2048]{2,1,0:T(2,128)(2,1)} %convert_element_type.48), calls=%async_computation.3 | async-start | bytes 131072 | tf_op jit(solution)/shard_map/all_to_all | solution.py:129
  111.2 4.8 %all-to-all-done.3 = bf16[8,2,2048]{2,1,0:T(2,128)(2,1)S(1)} async-done(((bf16[8,2,2048]{2,1,0:T(2,128)(2,1)}), bf16[8,2,2048]{2,1,0:T(2,128)(2,1)S(1)}, u32[]{:S(2)}, u32[]{:S(2)}) %all-to-all-start.3) | async-done | bytes 65568 | tf_op jit(solution)/shard_map/all_to_all | solution.py:129
  116.6 22.7 %all-gather.1 = bf16[8,4,2048]{2,1,0:T(4,128)(2,1)S(1)} all-gather(bf16[1,4,2048]{2,1,0:T(4,128)(2,1)S(1)} %bitcast.29), channel_id=2, replica_groups=mesh['group'=2,'dp'=4,'tensor'=4] {'group','dp'}, dimensions={0}, use_global_device_ids=true | all-gather | bytes 147456 | tf_op jit(solution)/shard_map/all_gather | solution.py:34
  139.3 3.7 %fusion.43 = f32[32,1024]{1,0:T(8,128)} fusion(bf16[32,2048]{1,0:T(8,128)(2,1)S(1)} %reshape.137, bf16[2048,1024]{1,0:T(8,128)(2,1)} %param.17), kind=kOutput, calls=%fused_computation.75 | convolution fusion | flops 134217728 | bytes 4456448 | tf_op jit(solution)/shard_map/dot_general | solution.py:33
  143.0 19.2 %reduce-scatter.3.cloned.1.call-done = f32[8,1024]{1,0:T(8,128)} async-done(((f32[32,1024]{1,0:T(8,128)}), f32[8,1024]{1,0:T(8,128)}) %reduce-scatter.3.cloned.1.call-update) | async-done | bytes 32784 | tf_op jit(solution)/shard_map/reduce_scatter | solution.py:38
  163.1 14.3 %psum.15 = f32[8]{0:T(128)S(1)} all-reduce(f32[8]{0:T(128)S(1)} %multiply_reduce_fusion), channel_id=1, replica_groups=mesh['group'=2,'dp'=4,'tensor'=4] {'group','dp'}, use_global_device_ids=true, to_apply=%region_10.11 | all-reduce | flops 8 | bytes 64 | tf_op jit(solution)/shard_map/psum | solution.py:14
  178.2 13.3 %all_gather.14 = bf16[32,1024]{1,0:T(8,128)(2,1)S(1)} all-gather(bf16[8,1024]{1,0:T(8,128)(2,1)S(1)} %multiply_convert_fusion), channel_id=1, replica_groups=mesh['group'=2,'dp'=4,'tensor'=4] {'tensor'}, dimensions={0}, use_global_device_ids=true | all-gather | bytes 81920 | tf_op jit(solution)/shard_map/all_gather | solution.py:20
  191.4 7.8 %fusion.44 = f32[32,7168]{1,0:T(8,128)S(1)} fusion(bf16[32,1024]{1,0:T(8,128)(2,1)S(1)} %all_gather.14, bf16[1024,7168]{1,0:T(8,128)(2,1)} %param.18), kind=kOutput, calls=%fused_computation.76 | convolution fusion | flops 469762048 | bytes 15663104 | tf_op jit(solution)/shard_map/dot_general | solution.py:23
  199.2 7.8 %fusion.45 = f32[32,7168]{1,0:T(8,128)S(1)} fusion(bf16[32,1024]{1,0:T(8,128)(2,1)S(1)} %all_gather.14, bf16[1024,7168]{1,0:T(8,128)(2,1)} %param.19), kind=kOutput, calls=%fused_computation.77 | convolution fusion | flops 469762048 | bytes 15663104 | tf_op jit(solution)/shard_map/dot_general | solution.py:23
  208.5 58.1 %all-reduce.5.cloned.1.call-done = f32[32,14336]{1,0:T(8,128)} async-done(((f32[32,14336]{1,0:T(8,128)}), f32[32,14336]{1,0:T(8,128)}) %all-reduce.5.cloned.1.call-update) | async-done | bytes 1835024
  267.8 23.6 %all-gather.2 = bf16[8,4,7168]{2,1,0:T(4,128)(2,1)S(1)} all-gather(bf16[1,4,7168]{2,1,0:T(4,128)(2,1)S(1)} %fusion.20), channel_id=1, replica_groups=mesh['group'=2,'dp'=4,'tensor'=4] {'group','dp'}, dimensions={0}, use_global_device_ids=true | all-gather | bytes 516096 | tf_op jit(solution)/shard_map/all_gather | solution.py:34
  291.5 8.5 %fusion.46 = f32[32,1024]{1,0:T(8,128)} fusion(bf16[32,7168]{1,0:T(8,128)(2,1)S(1)} %reshape.139, bf16[7168,1024]{1,0:T(8,128)(2,1)} %param.20), kind=kOutput, calls=%fused_computation.78 | convolution fusion | flops 469762048 | bytes 15269888 | tf_op jit(solution)/shard_map/dot_general | solution.py:33
  300.0 19.9 %reduce-scatter.5.cloned.1.call-done = f32[8,1024]{1,0:T(8,128)} async-done(((f32[32,1024]{1,0:T(8,128)}), f32[8,1024]{1,0:T(8,128)}) %reduce-scatter.5.cloned.1.call-update) | async-done | bytes 32784 | tf_op jit(solution)/shard_map/reduce_scatter | solution.py:38
  (66 shorter events, 17.8 us)
Async XLA Ops:
  6.5 83.9 %copy-start = (bf16[4,2,256,256]{3,2,1,0:T(8,128)(2,1)S(1)}, bf16[4,2,256,256]{3,2,1,0:T(8,128)(2,1)}, u32[]{:S(2)}) copy-start(bf16[4,2,256,256]{3,2,1,0:T(8,128)(2,1)} %param.21) | copy-start | bytes 3145732
  6.5 74.5 %copy-start.7 = (u32[32]{0:T(128)S(1)}, u32[32]{0:T(128)}, u32[]{:S(2)}) copy-start(u32[32]{0:T(128)} %constant.72) | copy-start | bytes 388
  6.5 40.7 %copy-start.3 = (bf16[1024,512]{1,0:T(8,128)(2,1)S(1)}, bf16[1024,512]{1,0:T(8,128)(2,1)}, u32[]{:S(2)}) copy-start(bf16[1024,512]{1,0:T(8,128)(2,1)} %param.16) | copy-start | bytes 3145732
  6.5 83.2 %copy-start.2 = (s32[4]{0:T(128)S(1)}, s32[4]{0:T(128)}, u32[]{:S(2)}) copy-start(s32[4]{0:T(128)} %param.22) | copy-start | bytes 52
  8.6 76.3 %all-to-all-start = ((s32[8,1,2]{2,1,0:T(1,128)}), s32[8,1,2]{2,1,0:T(1,128)S(1)}, u32[]{:S(2)}, u32[]{:S(2)}) async-start(s32[8,1,2]{2,1,0:T(1,128)} %bitcast), calls=%async_computation | async-start | bytes 8192 | tf_op jit(solution)/shard_map/all_to_all | solution.py:118
  85.0 8.2 %all-to-all-start.2 = ((bf16[8,2,512]{2,1,0:T(2,128)(2,1)}), bf16[8,2,512]{2,1,0:T(2,128)(2,1)S(1)}, u32[]{:S(2)}, u32[]{:S(2)}) async-start(bf16[8,2,512]{2,1,0:T(2,128)(2,1)} %reshape.81), calls=%async_computation.2 | async-start | bytes 32768 | tf_op jit(solution)/shard_map/all_to_all | solution.py:117
  93.2 9.0 %all-to-all-start.1 = ((bf16[8,2,2048]{2,1,0:T(2,128)(2,1)}), bf16[8,2,2048]{2,1,0:T(2,128)(2,1)S(1)}, u32[]{:S(2)}, u32[]{:S(2)}) async-start(bf16[8,2,2048]{2,1,0:T(2,128)(2,1)} %reshape.80), calls=%async_computation.1 | async-start | bytes 131072 | tf_op jit(solution)/shard_map/all_to_all | solution.py:116
  105.1 57.1 %copy-start.4 = (bf16[8,1024]{1,0:T(8,128)(2,1)S(1)}, bf16[8,1024]{1,0:T(8,128)(2,1)}, u32[]{:S(2)}) copy-start(bf16[8,1024]{1,0:T(8,128)(2,1)} %param.12) | copy-start | bytes 49156
  105.1 58.0 %copy-start.6 = (bf16[1024]{0:T(1024)(128)(2,1)S(1)}, bf16[1024]{0:T(1024)(128)(2,1)}, u32[]{:S(2)}) copy-start(bf16[1024]{0:T(1024)(128)(2,1)} %param.14) | copy-start | bytes 6148
  107.8 8.2 %all-to-all-start.3 = ((bf16[8,2,2048]{2,1,0:T(2,128)(2,1)}), bf16[8,2,2048]{2,1,0:T(2,128)(2,1)S(1)}, u32[]{:S(2)}, u32[]{:S(2)}) async-start(bf16[8,2,2048]{2,1,0:T(2,128)(2,1)} %convert_element_type.48), calls=%async_computation.3 | async-start | bytes 131072 | tf_op jit(solution)/shard_map/all_to_all | solution.py:129
  111.1 51.0 %reduce-scatter.3.cloned.1.call-start = ((), (), s32[]{:S(2)}) async-start(), calls=%async_computation.6 | async-start | bytes 163840 | tf_op jit(solution)/shard_map/reduce_scatter | solution.py:38
  143.0 123.6 %all-reduce.5.cloned.1.call-start = ((), (), s32[]{:S(2)}) async-start(), calls=%async_computation.8 | async-start | bytes 3670016
  208.4 111.5 %reduce-scatter.5.cloned.1.call-start = ((), (), s32[]{:S(2)}) async-start(), calls=%async_computation.7 | async-start | bytes 163840 | tf_op jit(solution)/shard_map/reduce_scatter | solution.py:38
  291.5 28.5 %copy-start.5 = (f32[8,1024]{1,0:T(8,128)S(1)}, f32[8,1024]{1,0:T(8,128)}, u32[]{:S(2)}) copy-start(f32[8,1024]{1,0:T(8,128)} %reduce-scatter.3.cloned.1.call-done) | copy-start | bytes 98308
  291.5 29.9 %copy-start.1 = (bf16[4,2,256,256]{3,2,1,0:T(8,128)(2,1)S(1)}, bf16[4,2,256,256]{3,2,1,0:T(8,128)(2,1)}, u32[]{:S(2)}) copy-start(bf16[4,2,256,256]{3,2,1,0:T(8,128)(2,1)} %param.21) | copy-start | bytes 3145732
Sparse Core Ops, SparseCore 0:
  143.1 19.0 reduce-scatter.2
  208.5 58.0 all-reduce.4
  300.1 19.7 reduce-scatter.4
where the time goes:
time: 329 us; the launch traced here: 328 us
  blocking collectives  135 us (41%)
  waiting for transfers between devices  107 us (33%)
  matrix products  35.6 us (11%)
  starting transfers between devices  16.1 us (5%)
  between operations  14 us (4%)
  local copies, waits for them, and re-layouts  10 us (3%)
  other arithmetic  9.91 us (3%)
    unnamed x4, waiting for transfers between devices  58.2 us
    all_gather x2, blocking collectives, project_rows(): lax.all_gather(local_rows, ('group', 'dp'), axis=0, tiled=True)  46.2 us
    reduce_scatter x2, waiting for transfers between devices, project_rows(): lax.psum_scatter(partial_sum, 'tensor', scatter_dimension=0, tiled=True)  39.1 us
    unnamed x1, blocking collectives  33.5 us
    psum x2, blocking collectives, normed(): squares = lax.psum(jnp.sum(values * values, axis=1), ('group', 'dp'))  29.1 us
    all_gather x2, blocking collectives, width_sum(): gathered = lax.all_gather(normal_rows, 'tensor', axis=0, tiled=True)  26.6 us
    dot_general x4, matrix products, width_sum(): jnp.dot(gathered, matrix, preferred_element_type=jnp.float32)  18.9 us
    dot_general x2, matrix products, project_rows(): jnp.dot(lax.all_gather(local_rows, ('group', 'dp'), axis=0, tiled=True),...  12.2 us
  transfers between devices with their start and end apart: 7, of which 5 were waited for; matrix products, arithmetic and copies ran while one was open for 4% of the time, Pallas kernels for 0%

commit v1 on v0

--- a/solution.py
+++ b/solution.py
@@ -4,7 +4,6 @@
 from jax.sharding import PartitionSpec as P
 
 D = 8192
-CAP = 2
 
 
 EPSILON = 1e-05
@@ -16,8 +15,10 @@
     return (values * scale[:, None] * gain.astype(jnp.float32)[None, :]).astype(jnp.bfloat16)
 
 
-def width_sum(normal_rows, matrices):
+def width_sum(normal_rows, matrices, order=None):
     gathered = lax.all_gather(normal_rows, "tensor", axis=0, tiled=True)
+    if order is not None:
+        gathered = permuted(order, gathered)
     return lax.psum_scatter(
         jnp.concatenate(
             [jnp.dot(gathered, matrix, preferred_element_type=jnp.float32) for matrix in matrices],
@@ -29,13 +30,16 @@
     )
 
 
-def project_rows(local_rows, matrix):
-    partial_sum = jnp.dot(
-        lax.all_gather(local_rows, ("group", "dp"), axis=0, tiled=True),
-        matrix,
-        preferred_element_type=jnp.float32,
-    )
+def project_rows(local_rows, matrix, order=None):
+    gathered = lax.all_gather(local_rows, ("group", "dp"), axis=0, tiled=True)
+    if order is not None:
+        gathered = permuted(order, gathered)
+    partial_sum = jnp.dot(gathered, matrix, preferred_element_type=jnp.float32)
     return lax.psum_scatter(partial_sum, "tensor", scatter_dimension=0, tiled=True)
+
+
+def permuted(order, rows):
+    return jnp.dot(order, rows, preferred_element_type=jnp.float32).astype(rows.dtype)
 
 
 def attend(query, fresh, stored, counts):
@@ -88,47 +92,18 @@
     lengths,
     location,
 ):
-    owners = lax.axis_size(("group", "dp"))
-    per_owner = cache.shape[0]
     resid = stream.astype(jnp.float32)
     attn_in = normed(resid, norm_attn)
-    joined = width_sum(attn_in, (w_query, w_keyval))
+    places = lax.all_gather(location, ("group", "dp"), axis=0, tiled=True)
+    slots = jnp.arange(places.shape[0], dtype=jnp.int32)
+    by_slot = (slots[:, None] == places[None, :]).astype(jnp.bfloat16)
+    by_request = (places[:, None] == slots[None, :]).astype(jnp.bfloat16)
+    joined = width_sum(attn_in, (w_query, w_keyval), by_slot)
     query_cols = w_query.shape[1]
     query = joined[:, :query_cols].astype(jnp.bfloat16)
     fresh = joined[:, query_cols:].astype(jnp.bfloat16)
-    fresh_cols = fresh.shape[1]
-    target = location // per_owner
-    place = target * CAP + location % per_owner % CAP
-    slot = location % per_owner
-    send_query = (
-        jnp.zeros((owners * CAP, query_cols), jnp.bfloat16)
-        .at[place]
-        .set(query)
-        .reshape(owners, CAP, query_cols)
-    )
-    send_fresh = (
-        jnp.zeros((owners * CAP, fresh_cols), jnp.bfloat16)
-        .at[place]
-        .set(fresh)
-        .reshape(owners, CAP, fresh_cols)
-    )
-    send_slot = jnp.zeros((owners * CAP,), jnp.int32).at[place].set(slot).reshape(owners, CAP)
-    got_query = lax.all_to_all(send_query, ("group", "dp"), split_axis=0, concat_axis=0, tiled=True)
-    got_fresh = lax.all_to_all(send_fresh, ("group", "dp"), split_axis=0, concat_axis=0, tiled=True)
-    got_slot = lax.all_to_all(send_slot, ("group", "dp"), split_axis=0, concat_axis=0, tiled=True)
-    sources = got_slot.shape[0]
-    count = got_slot.shape[1]
-    flat_slot = got_slot.reshape(-1)
-    answer = attend(
-        got_query.reshape(sources * count, -1),
-        got_fresh.reshape(sources * count, -1),
-        cache[flat_slot],
-        lengths[flat_slot],
-    )
-    answer = answer.reshape(sources, count, -1)
-    returned = lax.all_to_all(answer, ("group", "dp"), split_axis=0, concat_axis=0, tiled=True)
-    attended = returned.reshape(owners * CAP, -1)[place]
-    middle = resid + project_rows(attended, w_out)
+    attended = attend(query, fresh, cache, lengths)
+    middle = resid + project_rows(attended, w_out, by_request)
     ffn_in = normed(middle, norm_ffn)
     both = width_sum(ffn_in, (w_gate, w_up))
     hidden_cols = w_gate.shape[1]

time: 329 us -> 300 us (0.912)
  starting transfers between devices: 16.1 us -> 0.09 us
  blocking collectives: 135 us -> 144 us
  waiting for transfers between devices: 107 us -> 98 us
  local copies, waits for them, and re-layouts: 10 us -> 2.57 us
  matrix products: 35.6 us -> 32 us
    all_to_all x4 -> x0, starting transfers between devices: 16 us -> none  [the longest x1 5.17 us: per_device(): lax.all_to_all(send_slot, ('group', 'dp'), split_axis=0, concat_axis=0, t...]
    all_to_all x4 -> x0, waiting for transfers between devices: 9.67 us -> none  [the longest x1 4.89 us: per_device(): lax.all_to_all(send_query, ('group', 'dp'), split_axis=0, concat_axis=0,...]
    unnamed x1 -> x2, blocking collectives: 33.5 us -> 41.8 us
    gather x3 -> x0, local copies, waits for them, and re-layouts: 3.98 us -> none  [the longest x1 2.75 us: per_device(): cache[flat_slot]]
    dot_general x2 -> x3, matrix products: 12.2 us -> 12.4 us  [the longest x2 12.3 us: project_rows(): partial_sum = jnp.dot(gathered, matrix, preferred_element_type=jnp.float32)]
  transfers between devices with their start and end apart: 7 -> 3, of which waited for: 5 -> 3; matrix products, arithmetic and copies ran while one was open for 4% -> 0% of each run, Pallas kernels for 0% -> 0%
where the time goes in v1:
time: 300 us; the launch traced here: 299 us
  blocking collectives  144 us (48%)
  waiting for transfers between devices  98 us (33%)
  matrix products  32 us (11%)
  between operations  14.6 us (5%)
  other arithmetic  8.28 us (3%)
    unnamed x4, waiting for transfers between devices  58.2 us
    all_gather x2, blocking collectives, project_rows(): gathered = lax.all_gather(local_rows, ('group', 'dp'), axis=0, tiled=True)  46.8 us
    unnamed x2, blocking collectives  41.8 us
    reduce_scatter x2, waiting for transfers between devices, project_rows(): lax.psum_scatter(partial_sum, 'tensor', scatter_dimension=0, tiled=True)  39.9 us
    psum x2, blocking collectives, normed(): squares = lax.psum(jnp.sum(values * values, axis=1), ('group', 'dp'))  28.6 us
    all_gather x2, blocking collectives, width_sum(): gathered = lax.all_gather(normal_rows, 'tensor', axis=0, tiled=True)  26.6 us
    dot_general x4, matrix products, width_sum(): jnp.dot(gathered, matrix, preferred_element_type=jnp.float32)  18.9 us
    dot_general x2, matrix products, project_rows(): partial_sum = jnp.dot(gathered, matrix, preferred_element_type=jnp.float32)  12.3 us
  transfers between devices with their start and end apart: 3, of which 3 were waited for; matrix products, arithmetic and copies ran while one was open for 0% of the time, Pallas kernels for 0%

profile of v1, /device:TPU:0, one launch (start us, length us, event | category | flops | bytes accessed | tf_op | source)
XLA Modules:
  0.0 299.4 jit_solution(2769393561572899321)
XLA Ops:
  6.6 1.5 fusion.28
  8.7 0.9 dynamic-update-slice
  9.6 9.6 %all-reduce = s32[32]{0:T(128)S(1)} all-reduce(s32[32]{0:T(128)S(1)} %dynamic-update-slice), channel_id=1, replica_groups=mesh['group'=2,'dp'=4,'tensor'=4] {'group','dp'}, use_global_device_ids=true, to_apply=%add | all-reduce | flops 32 | bytes 256
  19.3 0.8 fusion.8
  20.8 14.3 %psum.14 = f32[8]{0:T(128)S(1)} all-reduce(f32[8]{0:T(128)S(1)} %fusion.8), channel_id=1, replica_groups=mesh['group'=2,'dp'=4,'tensor'=4] {'group','dp'}, use_global_device_ids=true, to_apply=%region_1.0 | all-reduce | flops 8 | bytes 64 | tf_op jit(solution)/shard_map/psum | solution.py:13
  35.8 13.4 %all_gather.16 = bf16[32,1024]{1,0:T(8,128)(2,1)S(1)} all-gather(bf16[8,1024]{1,0:T(8,128)(2,1)S(1)} %fusion.10), channel_id=1, replica_groups=mesh['group'=2,'dp'=4,'tensor'=4] {'tensor'}, dimensions={0}, use_global_device_ids=true | all-gather | bytes 81920 | tf_op jit(solution)/shard_map/all_gather | solution.py:19
  49.3 3.0 %fusion.29 = f32[32,2048]{1,0:T(8,128)S(1)} fusion(bf16[32,1024]{1,0:T(8,128)(2,1)S(1)} %convolution_convert_fusion.1, bf16[1024,2048]{1,0:T(8,128)(2,1)} %param.15), kind=kOutput, calls=%fused_computation.55 | convolution fusion | flops 134217728 | bytes 4521984 | tf_op jit(solution)/shard_map/dot_general | solution.py:24
  52.7 32.2 %all-reduce.7 = bf16[32,2560]{1,0:T(8,128)(2,1)S(1)} all-reduce(f32[32,2560]{1,0:T(8,128)S(1)} %pad_maximum_fusion.1), channel_id=2, replica_groups=mesh['group'=2,'dp'=4,'tensor'=4] {'group','dp'}, use_global_device_ids=true, to_apply=%region_2.0.clone | all-reduce | flops 81920 | bytes 491520
  86.6 23.3 %all-gather = bf16[8,4,2048]{2,1,0:T(4,128)(2,1)S(1)} all-gather(bf16[1,4,2048]{2,1,0:T(4,128)(2,1)S(1)} %reshape.45), channel_id=1, replica_groups=mesh['group'=2,'dp'=4,'tensor'=4] {'group','dp'}, dimensions={0}, use_global_device_ids=true | all-gather | bytes 147456 | tf_op jit(solution)/shard_map/all_gather | solution.py:34
  109.9 3.8 %fusion = f32[32,1024]{1,0:T(8,128)} fusion(bf16[2048,1024]{1,0:T(8,128)(2,1)} %param.17, bf16[32,2048]{1,0:T(8,128)(2,1)S(1)} %reshape.46, s32[32]{0:T(128)S(1)} %all-reduce), kind=kOutput, calls=%fused_computation.2 | convolution fusion | flops 138478592 | bytes 4456576 | tf_op jit(solution)/shard_map/dot_general | solution.py:37
  113.8 20.0 %reduce-scatter.3.cloned.1.call-done = f32[8,1024]{1,0:T(8,128)} async-done(((f32[32,1024]{1,0:T(8,128)}), f32[8,1024]{1,0:T(8,128)}) %reduce-scatter.3.cloned.1.call-update) | async-done | bytes 32784 | tf_op jit(solution)/shard_map/reduce_scatter | solution.py:38
  133.8 0.9 multiply_reduce_fusion
  134.7 14.3 %psum.15 = f32[8]{0:T(128)S(1)} all-reduce(f32[8]{0:T(128)S(1)} %multiply_reduce_fusion), channel_id=1, replica_groups=mesh['group'=2,'dp'=4,'tensor'=4] {'group','dp'}, use_global_device_ids=true, to_apply=%region_7.8 | all-reduce | flops 8 | bytes 64 | tf_op jit(solution)/shard_map/psum | solution.py:13
  149.0 0.8 multiply_convert_fusion
  149.8 13.3 %all_gather.18 = bf16[32,1024]{1,0:T(8,128)(2,1)S(1)} all-gather(bf16[8,1024]{1,0:T(8,128)(2,1)S(1)} %multiply_convert_fusion), channel_id=1, replica_groups=mesh['group'=2,'dp'=4,'tensor'=4] {'tensor'}, dimensions={0}, use_global_device_ids=true | all-gather | bytes 81920 | tf_op jit(solution)/shard_map/all_gather | solution.py:19
  163.1 7.8 %fusion.31 = f32[32,7168]{1,0:T(8,128)S(1)} fusion(bf16[32,1024]{1,0:T(8,128)(2,1)S(1)} %all_gather.18, bf16[1024,7168]{1,0:T(8,128)(2,1)} %param.18), kind=kOutput, calls=%fused_computation.57 | convolution fusion | flops 469762048 | bytes 15663104 | tf_op jit(solution)/shard_map/dot_general | solution.py:24
  170.9 7.8 %fusion.32 = f32[32,7168]{1,0:T(8,128)S(1)} fusion(bf16[32,1024]{1,0:T(8,128)(2,1)S(1)} %all_gather.18, bf16[1024,7168]{1,0:T(8,128)(2,1)} %param.19), kind=kOutput, calls=%fused_computation.58 | convolution fusion | flops 469762048 | bytes 15663104 | tf_op jit(solution)/shard_map/dot_general | solution.py:24
  178.7 1.4 pad_maximum_fusion
  180.1 58.1 %all-reduce.6.cloned.1.call-done = f32[32,14336]{1,0:T(8,128)} async-done(((f32[32,14336]{1,0:T(8,128)}), f32[32,14336]{1,0:T(8,128)}) %all-reduce.6.cloned.1.call-update) | async-done | bytes 1835024
  238.2 1.2 fusion.6
  239.4 23.6 %all-gather.1 = bf16[8,4,7168]{2,1,0:T(4,128)(2,1)S(1)} all-gather(bf16[1,4,7168]{2,1,0:T(4,128)(2,1)S(1)} %fusion.6), channel_id=1, replica_groups=mesh['group'=2,'dp'=4,'tensor'=4] {'group','dp'}, dimensions={0}, use_global_device_ids=true | all-gather | bytes 516096 | tf_op jit(solution)/shard_map/all_gather | solution.py:34
  263.1 8.4 %fusion.33 = f32[32,1024]{1,0:T(8,128)} fusion(bf16[32,7168]{1,0:T(8,128)(2,1)S(1)} %reshape.48, bf16[7168,1024]{1,0:T(8,128)(2,1)} %param.20), kind=kOutput, calls=%fused_computation.59 | convolution fusion | flops 469762048 | bytes 15269888 | tf_op jit(solution)/shard_map/dot_general | solution.py:37
  271.6 19.9 %reduce-scatter.5.cloned.1.call-done = f32[8,1024]{1,0:T(8,128)} async-done(((f32[32,1024]{1,0:T(8,128)}), f32[8,1024]{1,0:T(8,128)}) %reduce-scatter.5.cloned.1.call-update) | async-done | bytes 32784 | tf_op jit(solution)/shard_map/reduce_scatter | solution.py:38
  291.5 1.4 fusion.20
  (42 shorter events, 3.3 us)
Async XLA Ops:
  6.5 45.8 %copy-start = (bf16[1024,512]{1,0:T(8,128)(2,1)S(1)}, bf16[1024,512]{1,0:T(8,128)(2,1)}, u32[]{:S(2)}) copy-start(bf16[1024,512]{1,0:T(8,128)(2,1)} %param.16) | copy-start | bytes 3145732
  6.5 79.1 %copy-start.5 = (s32[4]{0:T(128)S(1)}, s32[4]{0:T(128)}, u32[]{:S(2)}) copy-start(s32[4]{0:T(128)} %param.22) | copy-start | bytes 52
  6.5 79.3 %copy-start.3 = (bf16[4,2,256,256]{3,2,1,0:T(8,128)(2,1)S(1)}, bf16[4,2,256,256]{3,2,1,0:T(8,128)(2,1)}, u32[]{:S(2)}) copy-start(bf16[4,2,256,256]{3,2,1,0:T(8,128)(2,1)} %param.21) | copy-start | bytes 3145732
  6.5 127.3 %reduce-scatter.3.cloned.1.call-start = ((), (), s32[]{:S(2)}) async-start(), calls=%async_computation.2 | async-start | bytes 163840 | tf_op jit(solution)/shard_map/reduce_scatter | solution.py:38
  52.6 81.2 %copy-start.1 = (bf16[8,1024]{1,0:T(8,128)(2,1)S(1)}, bf16[8,1024]{1,0:T(8,128)(2,1)}, u32[]{:S(2)}) copy-start(bf16[8,1024]{1,0:T(8,128)(2,1)} %param.12) | copy-start | bytes 49156
  52.6 82.0 %copy-start.4 = (bf16[1024]{0:T(1024)(128)(2,1)S(1)}, bf16[1024]{0:T(1024)(128)(2,1)}, u32[]{:S(2)}) copy-start(bf16[1024]{0:T(1024)(128)(2,1)} %param.14) | copy-start | bytes 6148
  113.8 124.4 %all-reduce.6.cloned.1.call-start = ((), (), s32[]{:S(2)}) async-start(), calls=%async_computation.4 | async-start | bytes 3670016
  180.1 111.4 %reduce-scatter.5.cloned.1.call-start = ((), (), s32[]{:S(2)}) async-start(), calls=%async_computation.3 | async-start | bytes 163840 | tf_op jit(solution)/shard_map/reduce_scatter | solution.py:38
  263.1 28.4 %copy-start.2 = (f32[8,1024]{1,0:T(8,128)S(1)}, f32[8,1024]{1,0:T(8,128)}, u32[]{:S(2)}) copy-start(f32[8,1024]{1,0:T(8,128)} %reduce-scatter.3.cloned.1.call-done) | copy-start | bytes 98308
Sparse Core Ops, SparseCore 0:
  113.9 19.8 reduce-scatter.2
  180.2 57.9 all-reduce.5
  271.7 19.7 reduce-scatter.4
